TPU v7x, 32 devices: a whole 2x2x4 slice. The times are simulated.
32 devices in a mesh: gx: 8 (over z, y), gy: 2 (over core), gz: 2 (over x).
Axes of the slice: x: 2, y: 2, z: 4, core: 2. Of those that a mesh axis runs over, the one named last changes fastest.
Arguments:
- velocity: float32 [3, 4, 64, 768], P(None, 'gz', 'gx', 'gy'), may hold values from -6 to 6
- adjoint: float32 [3, 4, 64, 768], P(None, 'gz', 'gx', 'gy'), may hold values from -0.3 to 0.3
- viscosity: float32 [4, 64, 768], P('gz', 'gx', 'gy'), may hold values from 0.5 to 5
- hang_flags: int32 [64, 256], P('gx', 'gy'), may hold values 0 or 1
- hang_index: int32 [64, 256], P('gx', 'gy'), may hold values from 0 to 7
- block_table: float32 [8, 3, 3], replicated, may hold values from -0.5 to 1
- friction: float32 [64, 768], P('gx', ('gy', 'gz')), may hold values from -3 to 3
- basal_mask: int32 [64, 768], P('gx', ('gy', 'gz')), may hold values 0 or 1
- direction: float32 [64, 768], P('gx', ('gy', 'gz')), may hold values from -6 to 6
Outputs:
- stokes_image: float32 [3, 4, 64, 768], P(None, 'gz', 'gx', 'gy')
- hessian_dir: float32 [64, 768], P('gx', ('gy', 'gz'))
All inputs are finite; a program needn't handle non-finite values. No bound on the sum of `hang_flags` or of `basal_mask` on one device may be relied on, other than what follows from the above.
Results may differ from a plain program's by a relative error of at most 0.00025.
Values sent between devices are 32-bit elements; how exact they have to be, the bound alone decides.
A program may use at most 64 MiB of HBM per device.

v0:
```python
import jax
import jax.numpy as jnp
from jax import lax
from jax.sharding import PartitionSpec as P

NB = 8


reg_weight = 0.05


def extended_2(cells, sides, width):
    for axis, dim in sides:
        count = lax.axis_size(axis)
        ends = count - 1
        head = lax.slice_in_dim(cells, 0, width, axis=dim)
        tail = lax.slice_in_dim(cells, cells.shape[dim] - width, cells.shape[dim], axis=dim)
        cells = jnp.concatenate(
            [
                lax.ppermute(tail, axis, [(i, (i + 1) % count) for i in range(ends)]),
                cells,
                lax.ppermute(head, axis, [((i + 1) % count, i) for i in range(ends)]),
            ],
            axis=dim,
        )
    return cells


def block_matrices(hang_flags, hang_index, block_table):
    blocks = jnp.zeros((3, 3) + hang_index.shape, jnp.float32)
    for number in range(NB):
        chosen = (hang_index == number).astype(jnp.float32)
        blocks = blocks + block_table[number][:, :, None, None] * chosen[None, None]
    hanging = hang_flags.astype(jnp.float32)
    identity = jnp.eye(3, dtype=jnp.float32)[:, :, None, None]
    return hanging * blocks + (1.0 - hanging) * identity


def apply_blocks(local_blocks, field, transpose):
    groups = field.shape[3] // 3
    shaped = field.reshape(field.shape[0], field.shape[1], field.shape[2], 3, groups)
    if transpose:
        mixed = jnp.einsum(
            "mkxg,czxmg->czxkg", local_blocks, shaped, precision=lax.Precision.HIGHEST
        )
    else:
        mixed = jnp.einsum(
            "mkxg,czxkg->czxmg", local_blocks, shaped, precision=lax.Precision.HIGHEST
        )
    return mixed.reshape(field.shape)


def shifted(padded, spatial, offset):
    lead = padded.ndim - 3
    index = [slice(None)] * lead + [slice(1, -1)] * 3
    if offset == 1:
        index[lead + spatial] = slice(2, None)
    elif offset == -1:
        index[lead + spatial] = slice(None, -2)
    return padded[tuple(index)]


def stencil(padded_vel, padded_visc):
    centre_vel = shifted(padded_vel, 0, 0)
    centre_visc = shifted(padded_visc, 0, 0)
    total = jnp.zeros(centre_vel.shape, jnp.float32)
    for spatial in range(3):
        for offset in (1, -1):
            face = 0.5 * (centre_visc + shifted(padded_visc, spatial, offset))
            total = total + face[None] * (centre_vel - shifted(padded_vel, spatial, offset))
    return total


def laplace(padded):
    return (
        4.0 * padded[1:-1, 1:-1]
        - padded[2:, 1:-1]
        - padded[:-2, 1:-1]
        - padded[1:-1, 2:]
        - padded[1:-1, :-2]
    )


def local(
    velocity,
    adjoint,
    viscosity,
    hang_flags,
    hang_index,
    block_table,
    friction,
    basal_mask,
    direction,
):
    local_blocks = block_matrices(hang_flags, hang_index, block_table)
    constrained = apply_blocks(local_blocks, velocity, False)
    stacked = jnp.concatenate([constrained, viscosity[None]], axis=0)
    padded = extended_2(stacked, (("gx", 2), ("gy", 3), ("gz", 1)), 1)
    applied = stencil(padded[:3], padded[3])
    stokes_image = apply_blocks(local_blocks, applied, True)
    partial_value = jnp.sum(stokes_image * adjoint, axis=(0, 1))
    column = lax.psum_scatter(partial_value, "gz", scatter_dimension=1, tiled=True)
    rim_deep = extended_2(direction, (("gx", 0), (("gy", "gz"), 1)), 2)
    extended = laplace(rim_deep)
    rows_dev = direction.shape[0]
    cols_dev = direction.shape[1]
    row_global = lax.axis_index("gx") * rows_dev - 1 + jnp.arange(rows_dev + 2, dtype=jnp.int32)
    col_global = (
        lax.axis_index(("gy", "gz")) * cols_dev - 1 + jnp.arange(cols_dev + 2, dtype=jnp.int32)
    )
    row_valid = (row_global >= 0) & (row_global < rows_dev * lax.axis_size("gx"))
    col_valid = (col_global >= 0) & (col_global < cols_dev * lax.axis_size(("gy", "gz")))
    inside = (row_valid[:, None] & col_valid[None, :]).astype(jnp.float32)
    bilaplace = laplace(extended * inside)
    hessian_dir = reg_weight * bilaplace + basal_mask.astype(jnp.float32) * (
        jnp.exp(friction) * column
    )
    return (stokes_image, hessian_dir)


def solution(mesh):
    return jax.shard_map(
        local,
        mesh=mesh,
        in_specs=(
            P(None, "gz", "gx", "gy"),
            P(None, "gz", "gx", "gy"),
            P("gz", "gx", "gy"),
            P("gx", "gy"),
            P("gx", "gy"),
            P(),
            P("gx", ("gy", "gz")),
            P("gx", ("gy", "gz")),
            P("gx", ("gy", "gz")),
        ),
        out_specs=(P(None, "gz", "gx", "gy"), P("gx", ("gy", "gz"))),
        check_vma=False,
    )
```

profile of v0, /device:TPU:0, one launch (start us, length us, event | category | flops | bytes accessed | tf_op | source)
XLA Modules:
  0.0 217.6 jit_solution(2325881880631126281)
XLA Ops:
  7.2 0.0 reduce-scatter.4.cloned.1.call-start
  7.2 0.7 broadcast_subtract_fusion
  7.9 0.7 convert_element_type.38
  8.6 0.7 compare_convert_fusion.7
  9.3 1.2 slice_reduce_fusion.7
  10.5 3.4 %copy.16 = f32[3,2,8,3,128]{3,0,1,4,2:T(4,128)} copy(f32[3,2,8,3,128]{4,2,3,1,0:T(8,128)} %bitcast.37) | data formatting | bytes 147456 | tf_op jit(solution)/shard_map/reshape | solution.py:41
  13.8 114.7 %convolution_bitcast_fusion.1 = f32[3,2,8,3,128]{0,3,1,4,2:T(4,128)} fusion(f32[3,2,8,3,128]{3,0,1,4,2:T(4,128)} %copy.16, f32[3,3]{1,0:T(4,128)S(1)} %fusion.39, f32[8,128]{1,0:T(8,128)S(1)} %broadcast_subtract_fusion, f32[8,128]{1,0:T(8,128)S(1)} %get-tuple-element.32, f32[3,3]{1,0:T(4,128)S(1)} %get-tuple-element.8, f32[8,128]{1,0:T(8,128)S(1)} %get-tuple-element.33, ...), kind=kOutput, calls=%fused_computation.1 | convolution fusion | flops 829440 | bytes 188740 | tf_op jit(solution)/shard_map/mkxg,czxkg->czxmg/dot_general | solution.py:47
  128.6 0.0 copy-start
  128.6 0.0 copy-start.2
  128.6 2.7 %copy.17 = f32[3,2,8,3,128]{4,2,3,1,0:T(8,128)S(1)} copy(f32[3,2,8,3,128]{0,3,1,4,2:T(4,128)} %convolution_bitcast_fusion.1) | data formatting | bytes 147456 | tf_op jit(solution)/shard_map/mkxg,czxkg->czxmg/transpose | solution.py:47
  131.3 0.0 copy-done
  131.3 4.9 %collective-permute-start = (f32[4,2,1,384]{3,2,1,0:T(1,128)S(1)}, f32[4,2,1,384]{3,2,1,0:T(1,128)S(1)}, u32[]{:S(2)}, u32[]{:S(2)}) collective-permute-start(f32[4,2,1,384]{3,2,1,0:T(1,128)S(1)} %get-tuple-element.20), channel_id=1, source_target_pairs={{0,4},{4,8},{8,12},{12,16},{16,20},{20,24},{24,28},{1,5},{5,9},{9,... | collective-permute-start | bytes 36872 | tf_op jit(solution)/shard_map/ppermute | solution.py:20
  136.2 1.3 collective-permute-start.1
  137.5 0.0 copy-done.2
  137.5 4.5 %collective-permute-start.6 = (f32[2,192]{1,0:T(2,128)S(1)}, f32[2,192]{1,0:T(2,128)S(1)}, u32[]{:S(2)}, u32[]{:S(2)}) collective-permute-start(f32[2,192]{1,0:T(2,128)S(1)} %get-tuple-element.24), channel_id=1, source_target_pairs={{0,4},{4,8},{8,12},{12,16},{16,20},{20,24},{24,28},{1,5},{5,9},{9,... | collective-permute-start | bytes 4616 | tf_op jit(solution)/shard_map/ppermute | solution.py:20
  142.1 1.3 collective-permute-start.7
  143.4 0.0 collective-permute-done.6
  143.4 4.5 %collective-permute-done.7 = f32[2,192]{1,0:T(2,128)S(1)} collective-permute-done((f32[2,192]{1,0:T(2,128)S(1)}, f32[2,192]{1,0:T(2,128)S(1)}, u32[]{:S(2)}, u32[]{:S(2)}) %collective-permute-start.7) | collective-permute-done | bytes 1568 | tf_op jit(solution)/shard_map/ppermute | solution.py:22
  148.0 0.0 collective-permute-done
  148.0 0.0 collective-permute-done.1
  148.0 0.1 pad_maximum_fusion.25
  148.1 1.3 collective-permute-start.2
  149.4 1.3 collective-permute-start.3
  150.7 0.1 fusion.41
  150.8 3.4 %collective-permute-start.8 = (f32[12,2]{1,0:T(8,128)S(1)}, f32[12,2]{1,0:T(8,128)S(1)}, u32[]{:S(2)}, u32[]{:S(2)}) collective-permute-start(f32[12,2]{1,0:T(8,128)S(1)} %get-tuple-element.23), channel_id=1, source_target_pairs={{0,1},{1,2},{2,3},{4,5},{5,6},{6,7},{8,9},{9,10},{10,11},{12,13},{... | collective-permute-start | bytes 296 | tf_op jit(solution)/shard_map/ppermute | solution.py:20
  154.2 1.3 collective-permute-start.9
  155.5 0.0 collective-permute-done.2
  155.5 0.0 collective-permute-done.3
  155.5 0.2 pad_maximum_fusion
  155.8 4.6 %collective-permute-start.4 = (f32[4,1,10,386]{3,2,1,0:T(8,128)S(1)}, f32[4,1,10,386]{3,2,1,0:T(8,128)S(1)}, u32[]{:S(2)}, u32[]{:S(2)}) collective-permute-start(f32[4,1,10,386]{3,2,1,0:T(8,128)S(1)} %get-tuple-element.11), channel_id=1, source_target_pairs={{0,1},{2,3},{4,5},{6,7},{8,9},{10,11},{12,13},{14,15},{16,17},{18,... | collective-permute-start | bytes 185288 | tf_op jit(solution)/shard_map/ppermute | solution.py:20
  160.3 1.3 collective-permute-start.5
  161.6 0.0 collective-permute-done.8
  161.7 0.0 collective-permute-done.9
  161.7 0.1 pad_maximum_fusion.36
  161.7 2.1 collective-permute-done.4
  163.8 4.1 %collective-permute-done.5 = f32[4,1,10,386]{3,2,1,0:T(8,128)S(1)} collective-permute-done((f32[4,1,10,386]{3,2,1,0:T(8,128)S(1)}, f32[4,1,10,386]{3,2,1,0:T(8,128)S(1)}, u32[]{:S(2)}, u32[]{:S(2)}) %collective-permute-start.5) | collective-permute-done | bytes 61792 | tf_op jit(solution)/shard_map/ppermute | solution.py:22
  167.9 0.1 fusion.9
  168.0 0.1 fusion.33
  168.1 0.2 fusion.13
  168.3 2.6 %copy.18 = f32[3,2,8,3,128]{3,0,1,4,2:T(4,128)} copy(f32[3,2,8,3,128]{4,2,3,1,0:T(8,128)S(1)} %fusion.13) | data formatting | bytes 147456 | tf_op jit(solution)/shard_map/reshape | solution.py:41
  171.0 22.7 %convolution_bitcast_fusion = f32[3,2,8,3,128]{3,0,1,4,2:T(4,128)} fusion(f32[3,2,8,3,128]{3,0,1,4,2:T(4,128)} %copy.18, f32[3,3]{1,0:T(4,128)S(1)} %fusion.39, f32[8,128]{1,0:T(8,128)S(1)} %broadcast_subtract_fusion, f32[8,128]{1,0:T(8,128)S(1)} %get-tuple-element.32, f32[3,3]{1,0:T(4,128)S(1)} %get-tuple-element.8, f32[8,128]{1,0:T(8,128)S(1)} %get-tuple-element.33, ...), kind=kOutput, calls=%fused_computation | convolution fusion | flops 829440 | bytes 188740 | tf_op jit(solution)/shard_map/mkxg,czxmg->czxkg/dot_general | solution.py:43
  193.7 0.0 copy-start.3
  193.7 0.0 copy-start.4
  193.7 0.0 copy-start.5
  193.7 2.7 %copy.19 = f32[3,2,8,3,128]{4,2,3,1,0:T(8,128)S(1)} copy(f32[3,2,8,3,128]{3,0,1,4,2:T(4,128)} %convolution_bitcast_fusion) | data formatting | bytes 147456 | tf_op jit(solution)/shard_map/mkxg,czxmg->czxkg/transpose | solution.py:43
  196.5 0.0 copy-done.3
  196.5 0.0 copy-start.1
  196.5 0.8 copy.21
  197.3 0.0 reduce-scatter.4.cloned.1.call-update
  197.3 0.1 fusion.35
  197.4 11.7 %reduce-scatter.4.cloned.1.call-done = f32[192,8]{1,0:T(8,128)} async-done(((f32[384,8]{1,0:T(8,128)}), f32[192,8]{1,0:T(8,128)}) %reduce-scatter.4.cloned.1.call-update) | async-done | bytes 6160
  209.1 0.9 copy.22
  210.1 0.0 copy-done.4
  210.1 0.0 copy-done.5
  210.1 0.7 fusion.38
  210.8 0.0 copy-done.1
  (8 shorter events, 0.1 us)
Async XLA Ops:
  7.2 202.0 %reduce-scatter.4.cloned.1.call-start = ((), (), s32[]{:S(2)}) async-start(), calls=%async_computation.1 | async-start | bytes 294912
  128.6 2.7 %copy-start = (f32[2,8,384]{2,1,0:T(8,128)S(1)}, f32[2,8,384]{2,1,0:T(8,128)}, u32[]{:S(2)}) copy-start(f32[2,8,384]{2,1,0:T(8,128)} %param.11) | copy-start | bytes 73732
  128.6 8.9 %copy-start.2 = (f32[8,192]{1,0:T(8,128)S(1)}, f32[8,192]{1,0:T(8,128)}, u32[]{:S(2)}) copy-start(f32[8,192]{1,0:T(8,128)} %param.17) | copy-start | bytes 18436
  131.3 16.7 %collective-permute-start = (f32[4,2,1,384]{3,2,1,0:T(1,128)S(1)}, f32[4,2,1,384]{3,2,1,0:T(1,128)S(1)}, u32[]{:S(2)}, u32[]{:S(2)}) collective-permute-start(f32[4,2,1,384]{3,2,1,0:T(1,128)S(1)} %get-tuple-element.20), channel_id=1, source_target_pairs={{0,4},{4,8},{8,12},{12,16},{16,20},{20,24},{24,28},{1,5},{5,9},{9,... | collective-permute-start | bytes 36872 | tf_op jit(solution)/shard_map/ppermute | solution.py:20
  136.2 11.8 %collective-permute-start.1 = (f32[4,2,1,384]{3,2,1,0:T(1,128)S(1)}, f32[4,2,1,384]{3,2,1,0:T(1,128)S(1)}, u32[]{:S(2)}, u32[]{:S(2)}) collective-permute-start(f32[4,2,1,384]{3,2,1,0:T(1,128)S(1)} %get-tuple-element.21), channel_id=1, source_target_pairs={{4,0},{8,4},{12,8},{16,12},{20,16},{24,20},{28,24},{5,1},{9,5},{13... | collective-permute-start | bytes 36872 | tf_op jit(solution)/shard_map/ppermute | solution.py:22
  137.5 5.9 %collective-permute-start.6 = (f32[2,192]{1,0:T(2,128)S(1)}, f32[2,192]{1,0:T(2,128)S(1)}, u32[]{:S(2)}, u32[]{:S(2)}) collective-permute-start(f32[2,192]{1,0:T(2,128)S(1)} %get-tuple-element.24), channel_id=1, source_target_pairs={{0,4},{4,8},{8,12},{12,16},{16,20},{20,24},{24,28},{1,5},{5,9},{9,... | collective-permute-start | bytes 4616 | tf_op jit(solution)/shard_map/ppermute | solution.py:20
  142.1 5.9 %collective-permute-start.7 = (f32[2,192]{1,0:T(2,128)S(1)}, f32[2,192]{1,0:T(2,128)S(1)}, u32[]{:S(2)}, u32[]{:S(2)}) collective-permute-start(f32[2,192]{1,0:T(2,128)S(1)} %get-tuple-element.25), channel_id=1, source_target_pairs={{4,0},{8,4},{12,8},{16,12},{20,16},{24,20},{28,24},{5,1},{9,5},{13... | collective-permute-start | bytes 4616 | tf_op jit(solution)/shard_map/ppermute | solution.py:22
  148.1 7.4 %collective-permute-start.2 = (f32[4,2,10,1]{3,2,1,0:T(8,128)S(1)}, f32[4,2,10,1]{3,2,1,0:T(8,128)S(1)}, u32[]{:S(2)}, u32[]{:S(2)}) collective-permute-start(f32[4,2,10,1]{3,2,1,0:T(8,128)S(1)} %get-tuple-element.19), channel_id=1, source_target_pairs={{0,2},{1,3},{4,6},{5,7},{8,10},{9,11},{12,14},{13,15},{16,18},{17,... | collective-permute-start | bytes 968 | tf_op jit(solution)/shard_map/ppermute | solution.py:20
  149.4 6.1 %collective-permute-start.3 = (f32[4,2,10,1]{3,2,1,0:T(8,128)S(1)}, f32[4,2,10,1]{3,2,1,0:T(8,128)S(1)}, u32[]{:S(2)}, u32[]{:S(2)}) collective-permute-start(f32[4,2,10,1]{3,2,1,0:T(8,128)S(1)} %get-tuple-element.18), channel_id=1, source_target_pairs={{2,0},{3,1},{6,4},{7,5},{10,8},{11,9},{14,12},{15,13},{18,16},{19,... | collective-permute-start | bytes 968 | tf_op jit(solution)/shard_map/ppermute | solution.py:22
  150.8 10.8 %collective-permute-start.8 = (f32[12,2]{1,0:T(8,128)S(1)}, f32[12,2]{1,0:T(8,128)S(1)}, u32[]{:S(2)}, u32[]{:S(2)}) collective-permute-start(f32[12,2]{1,0:T(8,128)S(1)} %get-tuple-element.23), channel_id=1, source_target_pairs={{0,1},{1,2},{2,3},{4,5},{5,6},{6,7},{8,9},{9,10},{10,11},{12,13},{... | collective-permute-start | bytes 296 | tf_op jit(solution)/shard_map/ppermute | solution.py:20
  154.2 7.5 %collective-permute-start.9 = (f32[12,2]{1,0:T(8,128)S(1)}, f32[12,2]{1,0:T(8,128)S(1)}, u32[]{:S(2)}, u32[]{:S(2)}) collective-permute-start(f32[12,2]{1,0:T(8,128)S(1)} %get-tuple-element.22), channel_id=1, source_target_pairs={{1,0},{2,1},{3,2},{5,4},{6,5},{7,6},{9,8},{10,9},{11,10},{13,12},{... | collective-permute-start | bytes 296 | tf_op jit(solution)/shard_map/ppermute | solution.py:22
  155.8 8.0 %collective-permute-start.4 = (f32[4,1,10,386]{3,2,1,0:T(8,128)S(1)}, f32[4,1,10,386]{3,2,1,0:T(8,128)S(1)}, u32[]{:S(2)}, u32[]{:S(2)}) collective-permute-start(f32[4,1,10,386]{3,2,1,0:T(8,128)S(1)} %get-tuple-element.11), channel_id=1, source_target_pairs={{0,1},{2,3},{4,5},{6,7},{8,9},{10,11},{12,13},{14,15},{16,17},{18,... | collective-permute-start | bytes 185288 | tf_op jit(solution)/shard_map/ppermute | solution.py:20
  160.3 7.6 %collective-permute-start.5 = (f32[4,1,10,386]{3,2,1,0:T(8,128)S(1)}, f32[4,1,10,386]{3,2,1,0:T(8,128)S(1)}, u32[]{:S(2)}, u32[]{:S(2)}) collective-permute-start(f32[4,1,10,386]{3,2,1,0:T(8,128)S(1)} %get-tuple-element.10), channel_id=1, source_target_pairs={{1,0},{3,2},{5,4},{7,6},{9,8},{11,10},{13,12},{15,14},{17,16},{19,... | collective-permute-start | bytes 185288 | tf_op jit(solution)/shard_map/ppermute | solution.py:22
  193.7 2.8 %copy-start.3 = (f32[3,2,8,384]{3,2,1,0:T(8,128)S(1)}, f32[3,2,8,384]{3,2,1,0:T(8,128)}, u32[]{:S(2)}) copy-start(f32[3,2,8,384]{3,2,1,0:T(8,128)} %param.10) | copy-start | bytes 221188
  193.7 16.4 %copy-start.4 = (f32[8,192]{1,0:T(8,128)S(1)}, f32[8,192]{1,0:T(8,128)}, u32[]{:S(2)}) copy-start(f32[8,192]{1,0:T(8,128)} %param.15) | copy-start | bytes 18436
  193.7 16.4 %copy-start.5 = (s32[8,192]{1,0:T(8,128)S(1)}, s32[8,192]{1,0:T(8,128)}, u32[]{:S(2)}) copy-start(s32[8,192]{1,0:T(8,128)} %param.16) | copy-start | bytes 18436
  196.5 14.3 %copy-start.1 = (f32[3,2,8,3,128]{4,2,3,1,0:T(8,128)}, f32[3,2,8,3,128]{4,2,3,1,0:T(8,128)S(1)}, u32[]{:S(2)}) copy-start(f32[3,2,8,3,128]{4,2,3,1,0:T(8,128)S(1)} %copy.19) | copy-start | bytes 221188
Sparse Core Ops, SparseCore 0:
  197.5 11.6 reduce-scatter.3
where the time goes:
time: 218 us
  matrix products  137 us (63%)
  starting transfers between devices  25.1 us (12%)
  waiting for transfers between devices  22.4 us (10%)
  local copies, waits for them, and re-layouts  14.5 us (7%)
  between operations  14.3 us (7%)
  other arithmetic  3.75 us (2%)
    dot_general x1, matrix products, apply_blocks(): jnp.einsum('mkxg,czxkg->czxmg', local_blocks, shaped, precision=lax.Preci...  115 us
    dot_general x1, matrix products, apply_blocks(): jnp.einsum('mkxg,czxmg->czxkg', local_blocks, shaped, precision=lax.Preci...  22.7 us
    ppermute x5, starting transfers between devices, extended_2(): lax.ppermute(tail, axis, [(i, (i + 1) % count) for i in range(ends)])  18.6 us
    unnamed x2, waiting for transfers between devices  11.7 us
    ppermute x5, waiting for transfers between devices, extended_2(): lax.ppermute(head, axis, [((i + 1) % count, i) for i in range(ends)])  8.67 us
    ppermute x5, starting transfers between devices, extended_2(): lax.ppermute(head, axis, [((i + 1) % count, i) for i in range(ends)])  6.46 us
    reshape x2, local copies, waits for them, and re-layouts, apply_blocks(): field.reshape(field.shape[0], field.shape[1], field.shape[2], 3, groups)  6.03 us
  transfers between devices with their start and end apart: 11, of which 4 were waited for; matrix products, arithmetic and copies ran while one was open for 0% of the time, Pallas kernels for 0%

commit v1 on v0

v1 whole, which is shorter than its diff:
```python
import functools

import jax
import jax.numpy as jnp
from jax import lax
from jax.experimental import pallas as pl
from jax.experimental.pallas import tpu as pltpu
from jax.sharding import PartitionSpec as P

NB = 8
REG = 0.05
MESH = pl.DeviceIdType.MESH
XU, XD, YL, YR, ZZ, CP, CC, PS = range(8)


def shift(value, by, axis):
    return pltpu.roll(value, by % value.shape[axis], axis)


def kernel(
    sizes,
    vel_h, adj_h, visc_h, flags_h, index_h, table, fric_h, mask_h, dir_h,
    out, hess,
    vel, adj, flags, index, fric, mask, direc,
    cons, xs_u, xs_d, xr_u, xr_d, zr, yr_l, yr_r, big, cs_p, cs_c, cr_p, cr_c, ps, pr,
    load_sem, send_sem, recv_sem,
):
    ngx, ngy, ngz = sizes
    gx, gy, gz = (lax.axis_index(axis) for axis in ("gx", "gy", "gz"))
    rows, cols = cons.shape[2], cons.shape[3]
    tiles = [slice(128 * m, 128 * (m + 1)) for m in range(3)]
    half = direc.shape[1]
    low = gz == 0
    has_u, has_d = gx > 0, gx < ngx - 1
    has_l, has_r = gy > 0, gy < ngy - 1
    has_c = jnp.where(low, gy, ngy - 1 - gy) > 0
    cross_gy = jnp.where(low, gy + ngy - 1, gy + 1) % ngy

    loads = [
        pltpu.make_async_copy(src, dst, load_sem.at[i])
        for i, (src, dst) in enumerate(
            (
                (vel_h, vel), (visc_h, cons.at[:, 3]), (flags_h, flags), (index_h, index),
                (dir_h, direc), (adj_h, adj), (fric_h, fric), (mask_h, mask),
            )
        )
    ]
    for load in loads:
        load.start()

    up = {"gx": (gx + ngx - 1) % ngx}
    down = {"gx": (gx + 1) % ngx}
    left = {"gy": (gy + ngy - 1) % ngy}
    right = {"gy": (gy + 1) % ngy}
    partner = {"gz": 1 - gz}
    cross = {"gy": cross_gy, "gz": 1 - gz}
    greet = ((has_u, up), (has_d, down), (has_l, left), (has_r, right), (has_c, cross))

    barrier = pltpu.get_barrier_semaphore()
    pl.semaphore_signal(barrier, inc=1, device_id=partner, device_id_type=MESH)
    for has, device in greet:
        @pl.when(has)
        def _():
            pl.semaphore_signal(barrier, inc=1, device_id=device, device_id_type=MESH)

    def remote(src, dst, at, device):
        return pltpu.make_async_remote_copy(
            src_ref=src, dst_ref=dst, send_sem=send_sem.at[at], recv_sem=recv_sem.at[at],
            device_id=device, device_id_type=MESH,
        )

    to_xu = remote(xs_d, xr_u, XU, down)
    to_xd = remote(xs_u, xr_d, XD, up)
    to_yl = remote(cons.at[:, :, :, cols - 128:], yr_l, YL, right)
    to_yr = remote(cons.at[:, :, :, :128], yr_r, YR, left)
    to_z = remote(cons.at[1 - gz], zr, ZZ, partner)
    to_cp = remote(cs_p, cr_p, CP, partner)
    to_cc = remote(cs_c, cr_c, CC, cross)
    to_ps = remote(ps, pr, PS, partner)

    for load in loads[:5]:
        load.wait()
    hanging = flags[...] == 1
    number = index[...]
    chosen = [number == n for n in range(NB)]
    block = [[None] * 3 for _ in range(3)]
    for m in range(3):
        for k in range(3):
            value = jnp.full(number.shape, table[m, k, 0], jnp.float32)
            for n in range(1, NB):
                value = jnp.where(chosen[n], table[m, k, n], value)
            block[m][k] = jnp.where(hanging, value, 1.0 if m == k else 0.0)
    for z in range(2):
        for c in range(3):
            slots = [vel[c, z, :, tile] for tile in tiles]
            for m in range(3):
                cons[z, c, :, tiles[m]] = (
                    block[m][0] * slots[0] + block[m][1] * slots[1] + block[m][2] * slots[2]
                )
    for z in range(2):
        for c in range(4):
            at = 4 * z + c
            xs_u[at:at + 1, :cols] = cons[z, c, 0:1, :]
            xs_d[at:at + 1, :cols] = cons[z, c, rows - 1:rows, :]
    for r in range(2):
        for send, row in ((xs_u, r), (xs_d, rows - 2 + r)):
            send[2 * r:2 * r + 1, cols:cols + 128] = direc[row:row + 1, :128]
            send[2 * r + 1:2 * r + 2, cols:cols + half - 128] = direc[row:row + 1, 128:]

    waits = sum((has.astype(jnp.int32) for has, _ in greet), jnp.int32(1))
    pl.semaphore_wait(barrier, waits)
    to_z.start()
    for has, copy in ((has_d, to_xu), (has_u, to_xd), (has_r, to_yl), (has_l, to_yr)):
        @pl.when(has)
        def _():
            copy.start()

    big[...] = jnp.zeros_like(big)
    for has, copy, buffer in ((has_u, to_xu, xr_u), (has_d, to_xd, xr_d)):
        @pl.when(has)
        def _():
            copy.wait_recv()

        @pl.when(jnp.logical_not(has))
        def _():
            buffer[...] = jnp.zeros_like(buffer)
    big[rows:2 * rows, 128:128 + half] = direc[...]
    for buffer, row in ((xr_u, rows - 2), (xr_d, 2 * rows)):
        for r in range(2):
            big[row + r:row + r + 1, 128:256] = buffer[2 * r:2 * r + 1, cols:cols + 128]
            big[row + r:row + r + 1, 256:128 + half] = (
                buffer[2 * r + 1:2 * r + 2, cols:cols + half - 128]
            )
    wide = big[...]
    edge_low, edge_high = wide[:, 128:256], wide[:, half:half + 128]
    cs_p[...] = jnp.where(low, edge_high, edge_low)
    cs_c[...] = jnp.where(low, edge_low, edge_high)
    to_cp.start()

    @pl.when(has_c)
    def _():
        to_cc.start()

    for has, copy, buffer in ((has_l, to_yl, yr_l), (has_r, to_yr, yr_r)):
        @pl.when(has)
        def _():
            copy.wait_recv()

        @pl.when(jnp.logical_not(has))
        def _():
            buffer[...] = jnp.zeros_like(buffer)
    to_z.wait_recv()
    for load in loads[5:]:
        load.wait()

    row_at = lax.broadcasted_iota(jnp.int32, (rows, cols), 0)
    own = [[cons[z, c] for c in range(4)] for z in range(2)]
    layer = [zr[c] for c in range(4)]
    below = [jnp.where(low, 0.0, a) for a in layer]
    above = [jnp.where(low, a, 0.0) for a in layer]
    stack = [below, own[0], own[1], above]
    total = [[None] * 3 for _ in range(2)]
    z_visc = [stack[i][3] + stack[i + 1][3] for i in range(3)]
    for c in range(3):
        flux = [z_visc[i] * (stack[i + 1][c] - stack[i][c]) for i in range(3)]
        for z in range(2):
            total[z][c] = flux[z] - flux[z + 1]
    for z in range(2):
        up_of, down_of, ext, ext_next = [], [], [], []
        for c in range(4):
            at = 4 * z + c
            a = own[z][c]
            up_of.append(jnp.where(row_at == 0, xr_u[at:at + 1, :cols], shift(a, 1, 0)))
            down_of.append(jnp.where(row_at == rows - 1, xr_d[at:at + 1, :cols], shift(a, -1, 0)))
            wide_a = jnp.concatenate([yr_l[z, c], a, yr_r[z, c]], axis=1)
            ext.append(wide_a)
            ext_next.append(shift(wide_a, -1, 1))
        visc_u, visc_d = own[z][3] + up_of[3], own[z][3] + down_of[3]
        visc_y = ext[3] + ext_next[3]
        for c in range(3):
            a = own[z][c]
            flux = visc_y * (ext[c] - ext_next[c])
            total[z][c] = 0.5 * (
                total[z][c]
                + visc_u * (a - up_of[c])
                + visc_d * (a - down_of[c])
                + (flux - shift(flux, 1, 1))[:, 128:128 + cols]
            )
    sums = [None] * 3
    for z in range(2):
        for c in range(3):
            for k in range(3):
                image = (
                    block[0][k] * total[z][c][:, tiles[0]]
                    + block[1][k] * total[z][c][:, tiles[1]]
                    + block[2][k] * total[z][c][:, tiles[2]]
                )
                out[c, z, :, tiles[k]] = image
                term = image * adj[c, z, :, tiles[k]]
                sums[k] = term if sums[k] is None else sums[k] + term
    sums = jnp.concatenate(sums, axis=1)
    first, second = sums[:, :half], sums[:, half:]
    ps[...] = jnp.where(low, second, first)
    to_ps.start()
    mine = jnp.where(low, first, second)

    to_cp.wait_recv()

    @pl.when(has_c)
    def _():
        to_cc.wait_recv()

    @pl.when(jnp.logical_not(has_c))
    def _():
        cr_c[...] = jnp.zeros_like(cr_c)

    from_p, from_c = cr_p[...], cr_c[...]
    from_low = jnp.where(low, from_c, from_p)
    from_high = shift(jnp.where(low, from_p, from_c), half % 128, 1)
    lane = lax.broadcasted_iota(jnp.int32, from_low.shape, 1)
    wide = jnp.concatenate(
        [from_low, wide[:, 128:256], jnp.where(lane < half % 128, wide[:, 256:], from_high)], axis=1
    )

    def laplace(v):
        return 4.0 * v - shift(v, 1, 0) - shift(v, -1, 0) - shift(v, 1, 1) - shift(v, -1, 1)

    row_g = gx * rows - rows + lax.broadcasted_iota(jnp.int32, wide.shape, 0)
    col_g = (gy * ngz + gz) * half - 128 + lax.broadcasted_iota(jnp.int32, wide.shape, 1)
    inside = (row_g >= 0) & (row_g < ngx * rows) & (col_g >= 0) & (col_g < ngy * ngz * half)
    twice = laplace(jnp.where(inside, laplace(wide), 0.0))[rows:2 * rows, 128:128 + half]
    scale = mask[...].astype(jnp.float32) * jnp.exp(fric[...])

    to_ps.wait_recv()
    hess[...] = REG * twice + scale * (mine + pr[...])

    for copy in (to_z, to_cp, to_ps):
        copy.wait_send()
    for has, copy in (
        (has_d, to_xu), (has_u, to_xd), (has_r, to_yl), (has_l, to_yr), (has_c, to_cc)
    ):
        @pl.when(has)
        def _():
            copy.wait_send()


def local(sizes, velocity, adjoint, viscosity, hang_flags, hang_index, block_table, friction, basal_mask, direction):
    _, levels, rows, cols = velocity.shape
    assert levels == 2 and sizes[2] == 2 and cols == 384
    half = direction.shape[1]
    f32 = jnp.float32
    vmem = pltpu.VMEM
    anywhere = pl.BlockSpec(memory_space=pl.ANY)
    return pl.pallas_call(
        functools.partial(kernel, sizes),
        out_shape=(
            jax.ShapeDtypeStruct(velocity.shape, f32),
            jax.ShapeDtypeStruct(direction.shape, f32),
        ),
        in_specs=[anywhere] * 5 + [pl.BlockSpec(memory_space=pltpu.SMEM)] + [anywhere] * 3,
        out_specs=(pl.BlockSpec(memory_space=vmem),) * 2,
        scratch_shapes=[
            vmem(velocity.shape, f32),
            vmem(velocity.shape, f32),
            vmem(hang_flags.shape, jnp.int32),
            vmem(hang_index.shape, jnp.int32),
            vmem(direction.shape, f32),
            vmem(direction.shape, jnp.int32),
            vmem(direction.shape, f32),
            vmem((levels, 4, rows, cols), f32),
            vmem((8, cols + 128), f32),
            vmem((8, cols + 128), f32),
            vmem((8, cols + 128), f32),
            vmem((8, cols + 128), f32),
            vmem((4, rows, cols), f32),
            vmem((levels, 4, rows, 128), f32),
            vmem((levels, 4, rows, 128), f32),
            vmem((3 * rows, 384), f32),
            vmem((3 * rows, 128), f32),
            vmem((3 * rows, 128), f32),
            vmem((3 * rows, 128), f32),
            vmem((3 * rows, 128), f32),
            vmem(direction.shape, f32),
            vmem(direction.shape, f32),
            pltpu.SemaphoreType.DMA((8,)),
            pltpu.SemaphoreType.DMA((8,)),
            pltpu.SemaphoreType.DMA((8,)),
        ],
        compiler_params=pltpu.CompilerParams(collective_id=0, has_side_effects=True),
        cost_estimate=pl.CostEstimate(flops=200_000, bytes_accessed=400_000, transcendentals=1536),
        name="hessian_apply",
    )(velocity, adjoint, viscosity, hang_flags, hang_index, jnp.transpose(block_table, (1, 2, 0)), friction, basal_mask, direction)


def solution(mesh):
    sizes = tuple(mesh.shape[axis] for axis in ("gx", "gy", "gz"))
    return jax.shard_map(
        functools.partial(local, sizes),
        mesh=mesh,
        in_specs=(
            P(None, "gz", "gx", "gy"),
            P(None, "gz", "gx", "gy"),
            P("gz", "gx", "gy"),
            P("gx", "gy"),
            P("gx", "gy"),
            P(),
            P("gx", ("gy", "gz")),
            P("gx", ("gy", "gz")),
            P("gx", ("gy", "gz")),
        ),
        out_specs=(P(None, "gz", "gx", "gy"), P("gx", ("gy", "gz"))),
        check_vma=False,
    )
```

time: 218 us -> 14.5 us (0.07)
  matrix products: 137 us -> 0 us
  starting transfers between devices: 25.1 us -> 0 us
  waiting for transfers between devices: 22.4 us -> 0 us
  between operations: 14.3 us -> 0.65 us
  local copies, waits for them, and re-layouts: 14.5 us -> 2.13 us
  Pallas kernels: 0 us -> 11.5 us
  other arithmetic: 3.75 us -> 0 us
    dot_general x2 -> x0, matrix products: 137 us -> none  [the longest x1 115 us: apply_blocks(): jnp.einsum('mkxg,czxkg->czxmg', local_blocks, shaped, precision=lax.Preci...]
    ppermute x10 -> x0, starting transfers between devices: 25.1 us -> none  [the longest x5 18.6 us: extended_2(): lax.ppermute(tail, axis, [(i, (i + 1) % count) for i in range(ends)])]
    unnamed x2 -> x0, waiting for transfers between devices: 11.7 us -> none
    pallas_call x0 -> x1, Pallas kernels: none -> 11.5 us  [local(): pl.pallas_call(functools.partial(kernel, sizes), out_shape=(jax.ShapeDtyp...]
    ppermute x10 -> x0, waiting for transfers between devices: 10.7 us -> none  [the longest x5 8.67 us: extended_2(): lax.ppermute(head, axis, [((i + 1) % count, i) for i in range(ends)])]
    reshape x2 -> x0, local copies, waits for them, and re-layouts: 6.03 us -> none  [apply_blocks(): field.reshape(field.shape[0], field.shape[1], field.shape[2], 3, groups)]
    transpose x2 -> x0, local copies, waits for them, and re-layouts: 5.45 us -> none  [the longest x1 2.74 us: apply_blocks(): jnp.einsum('mkxg,czxmg->czxkg', local_blocks, shaped, precision=lax.Preci...]
  transfers between devices with their start and end apart: 11 -> 0, of which waited for: 4 -> 0; matrix products, arithmetic and copies ran while one was open for 0% -> 0% of each run, Pallas kernels for 0% -> 0%
where the time goes in v1:
time: 14.5 us; the launch traced here: 14.2 us
  Pallas kernels  11.5 us (79%)
  local copies, waits for them, and re-layouts  2.13 us (15%)
  between operations  0.65 us (4%)
    pallas_call x1, Pallas kernels, local(): pl.pallas_call(functools.partial(kernel, sizes), out_shape=(jax.ShapeDtyp...  11.5 us
    unnamed x4, local copies, waits for them, and re-layouts  2.13 us

profile of v1, /device:TPU:0, one launch (start us, length us, event | category | flops | bytes accessed | tf_op | source)
XLA Modules:
  0.0 14.2 jit_solution(17248580262754946205)
XLA Ops:
  0.6 11.5 %hessian_apply.1 = (f32[3,2,8,384]{3,2,1,0:T(8,128)}, f32[8,192]{1,0:T(8,128)}) custom-call(f32[3,2,8,384]{3,2,1,0:T(8,128)} %vel_h.1, f32[3,2,8,384]{3,2,1,0:T(8,128)} %adj_h.1, f32[2,8,384]{2,1,0:T(8,128)} %visc_h.1, s32[8,128]{1,0:T(8,128)} %flags_h.1, s32[8,128]{1,0:T(8,128)} %index_h.1, f32[3,3,8]{2,1,0:T(4,128)} %bitcast.1, f32[8,192]{1,0:T(8,128)} %fric_h.1, ...), custom_call_target="tpu_custom_call" | custom-call | flops 200000 | bytes 400000 | tf_op jit(solution)/shard_map/hessian_apply/pallas_call | solution.py:254
  12.1 0.0 copy-start
  12.1 1.5 %copy.13 = f32[3,2,8,384]{3,2,1,0:T(8,128)} copy(f32[3,2,8,384]{3,2,1,0:T(8,128)} %get-tuple-element.4) | data formatting | bytes 147456
  13.6 0.0 copy-done
  13.6 0.6 %copy.14 = f32[8,192]{1,0:T(8,128)} copy(f32[8,192]{1,0:T(8,128)S(1)} %copy-done) | data formatting | bytes 12288
Async XLA Ops:
  12.1 1.5 %copy-start = (f32[8,192]{1,0:T(8,128)S(1)}, f32[8,192]{1,0:T(8,128)}, u32[]{:S(2)}) copy-start(f32[8,192]{1,0:T(8,128)} %get-tuple-element.5) | copy-start | bytes 18436

commit v2 on v1

--- a/solution.py
+++ b/solution.py
@@ -9,6 +9,7 @@
 
 NB = 8
 REG = 0.05
+LIMIT = 4 * 1024 * 1024
 MESH = pl.DeviceIdType.MESH
 XU, XD, YL, YR, ZZ, CP, CC, PS = range(8)
 
@@ -19,9 +20,9 @@
 
 def kernel(
     sizes,
-    vel_h, adj_h, visc_h, flags_h, index_h, table, fric_h, mask_h, dir_h,
+    vel_h, adj_h, visc_h, flags_h, index_h, table_h, fric_h, mask_h, dir_h,
     out, hess,
-    vel, adj, flags, index, fric, mask, direc,
+    table, vel, adj, flags, index, fric, mask, direc,
     cons, xs_u, xs_d, xr_u, xr_d, zr, yr_l, yr_r, big, cs_p, cs_c, cr_p, cr_c, ps, pr,
     load_sem, send_sem, recv_sem,
 ):
@@ -40,7 +41,7 @@
         pltpu.make_async_copy(src, dst, load_sem.at[i])
         for i, (src, dst) in enumerate(
             (
-                (vel_h, vel), (visc_h, cons.at[:, 3]), (flags_h, flags), (index_h, index),
+                (table_h, table), (flags_h, flags), (index_h, index), (vel_h, vel), (visc_h, cons.at[:, 3]),
                 (dir_h, direc), (adj_h, adj), (fric_h, fric), (mask_h, mask),
             )
         )
@@ -78,7 +79,7 @@
     to_cc = remote(cs_c, cr_c, CC, cross)
     to_ps = remote(ps, pr, PS, partner)
 
-    for load in loads[:5]:
+    for load in loads[:6]:
         load.wait()
     hanging = flags[...] == 1
     number = index[...]
@@ -150,7 +151,7 @@
         def _():
             buffer[...] = jnp.zeros_like(buffer)
     to_z.wait_recv()
-    for load in loads[5:]:
+    for load in loads[6:]:
         load.wait()
 
     row_at = lax.broadcasted_iota(jnp.int32, (rows, cols), 0)
@@ -244,22 +245,38 @@
             copy.wait_send()
 
 
+def store(image_v, hess_v, image_h, hess_h, sem):
+    copies = [
+        pltpu.make_async_copy(image_v, image_h, sem.at[0]),
+        pltpu.make_async_copy(hess_v, hess_h, sem.at[1]),
+    ]
+    for copy in copies:
+        copy.start()
+    for copy in copies:
+        copy.wait()
+
+
 def local(sizes, velocity, adjoint, viscosity, hang_flags, hang_index, block_table, friction, basal_mask, direction):
     _, levels, rows, cols = velocity.shape
     assert levels == 2 and sizes[2] == 2 and cols == 384
     half = direction.shape[1]
     f32 = jnp.float32
     vmem = pltpu.VMEM
-    anywhere = pl.BlockSpec(memory_space=pl.ANY)
-    return pl.pallas_call(
+    anywhere = pl.BlockSpec(memory_space=pltpu.HBM)
+    arguments = [
+        pltpu.with_memory_space_constraint(array, pltpu.HBM)
+        for array in (
+            velocity, adjoint, viscosity, hang_flags, hang_index,
+            jnp.transpose(block_table, (1, 2, 0)), friction, basal_mask, direction,
+        )
+    ]
+    image, hess = pl.pallas_call(
         functools.partial(kernel, sizes),
-        out_shape=(
-            jax.ShapeDtypeStruct(velocity.shape, f32),
-            jax.ShapeDtypeStruct(direction.shape, f32),
-        ),
-        in_specs=[anywhere] * 5 + [pl.BlockSpec(memory_space=pltpu.SMEM)] + [anywhere] * 3,
+        out_shape=(vmem(velocity.shape, f32), vmem(direction.shape, f32)),
+        in_specs=[anywhere] * 9,
         out_specs=(pl.BlockSpec(memory_space=vmem),) * 2,
         scratch_shapes=[
+            pltpu.SMEM((3, 3, NB), f32),
             vmem(velocity.shape, f32),
             vmem(velocity.shape, f32),
             vmem(hang_flags.shape, jnp.int32),
@@ -282,14 +299,26 @@
             vmem((3 * rows, 128), f32),
             vmem(direction.shape, f32),
             vmem(direction.shape, f32),
-            pltpu.SemaphoreType.DMA((8,)),
+            pltpu.SemaphoreType.DMA((9,)),
             pltpu.SemaphoreType.DMA((8,)),
             pltpu.SemaphoreType.DMA((8,)),
         ],
-        compiler_params=pltpu.CompilerParams(collective_id=0, has_side_effects=True),
+        compiler_params=pltpu.CompilerParams(collective_id=0, has_side_effects=True, vmem_limit_bytes=LIMIT),
         cost_estimate=pl.CostEstimate(flops=200_000, bytes_accessed=400_000, transcendentals=1536),
         name="hessian_apply",
-    )(velocity, adjoint, viscosity, hang_flags, hang_index, jnp.transpose(block_table, (1, 2, 0)), friction, basal_mask, direction)
+    )(*arguments)
+    return pl.pallas_call(
+        store,
+        out_shape=(
+            jax.ShapeDtypeStruct(velocity.shape, f32),
+            jax.ShapeDtypeStruct(direction.shape, f32),
+        ),
+        in_specs=[pl.BlockSpec(memory_space=vmem)] * 2,
+        out_specs=(anywhere,) * 2,
+        scratch_shapes=[pltpu.SemaphoreType.DMA((2,))],
+        compiler_params=pltpu.CompilerParams(vmem_limit_bytes=LIMIT),
+        name="store",
+    )(image, hess)
 
 
 def solution(mesh):

time: 14.5 us -> 11.6 us (0.80)
  local copies, waits for them, and re-layouts: 2.13 us -> 0 us
  Pallas kernels: 11.5 us -> 10.7 us
    unnamed x4 -> x0, local copies, waits for them, and re-layouts: 2.13 us -> none
    pallas_call x1 -> x2, Pallas kernels: 11.5 us -> 10.7 us  [the longest x1 10.1 us: local(): pl.pallas_call(functools.partial(kernel, sizes), out_shape=(vmem(velocity...]
where the time goes in v2:
time: 11.6 us; the launch traced here: 11.4 us
  Pallas kernels  10.7 us (92%)
  between operations  0.64 us (6%)
    pallas_call x1, Pallas kernels, local(): pl.pallas_call(functools.partial(kernel, sizes), out_shape=(vmem(velocity...  10.1 us
    pallas_call x1, Pallas kernels, local(): pl.pallas_call(store, out_shape=(jax.ShapeDtypeStruct(velocity.shape, f32...  0.65 us

profile of v2, /device:TPU:0, one launch (start us, length us, event | category | flops | bytes accessed | tf_op | source)
XLA Modules:
  0.0 11.4 jit_solution(15864269994528985724)
XLA Ops:
  0.6 10.1 %hessian_apply.1 = (f32[3,2,8,384]{3,2,1,0:T(8,128)S(1)}, f32[8,192]{1,0:T(8,128)S(1)}) custom-call(f32[3,2,8,384]{3,2,1,0:T(8,128)} %vel_h.1, f32[3,2,8,384]{3,2,1,0:T(8,128)} %adj_h.1, f32[2,8,384]{2,1,0:T(8,128)} %visc_h.1, s32[8,128]{1,0:T(8,128)} %flags_h.1, s32[8,128]{1,0:T(8,128)} %index_h.1, f32[3,3,8]{2,1,0:T(4,128)} %bitcast.1, f32[8,192]{1,0:T(8,128)} %fric_h.1, ...), custom_call_target="tpu_custom_call" | custom-call | flops 200000 | bytes 400000 | tf_op jit(solution)/shard_map/hessian_apply/pallas_call | solution.py:273
  10.7 0.7 %store.1 = (f32[3,2,8,384]{3,2,1,0:T(8,128)}, f32[8,192]{1,0:T(8,128)}) custom-call(f32[3,2,8,384]{3,2,1,0:T(8,128)S(1)} %get-tuple-element.4.image_v, f32[8,192]{1,0:T(8,128)S(1)} %get-tuple-element.5.hess_v), custom_call_target="tpu_custom_call" | custom-call | tf_op jit(solution)/shard_map/store/pallas_call | solution.py:310

commit v3 on v2

--- a/solution.py
+++ b/solution.py
@@ -11,7 +11,7 @@
 REG = 0.05
 LIMIT = 4 * 1024 * 1024
 MESH = pl.DeviceIdType.MESH
-XU, XD, YL, YR, ZZ, CP, CC, PS = range(8)
+XU, XD, YL, YR, ZZ, ZV, CP, CC, PS = range(9)
 
 
 def shift(value, by, axis):
@@ -74,10 +74,17 @@
     to_xd = remote(xs_u, xr_d, XD, up)
     to_yl = remote(cons.at[:, :, :, cols - 128:], yr_l, YL, right)
     to_yr = remote(cons.at[:, :, :, :128], yr_r, YR, left)
-    to_z = remote(cons.at[1 - gz], zr, ZZ, partner)
+    near, far = 1 - gz, gz
+    to_z = remote(vel_h.at[:, near], zr.at[:3], ZZ, partner)
+    to_zv = remote(visc_h.at[near], zr.at[3], ZV, partner)
     to_cp = remote(cs_p, cr_p, CP, partner)
     to_cc = remote(cs_c, cr_c, CC, cross)
     to_ps = remote(ps, pr, PS, partner)
+
+    waits = sum((has.astype(jnp.int32) for has, _ in greet), jnp.int32(1))
+    pl.semaphore_wait(barrier, waits)
+    to_z.start()
+    to_zv.start()
 
     for load in loads[:6]:
         load.wait()
@@ -98,9 +105,9 @@
                 cons[z, c, :, tiles[m]] = (
                     block[m][0] * slots[0] + block[m][1] * slots[1] + block[m][2] * slots[2]
                 )
-    for z in range(2):
+    for i, z in enumerate((near, far)):
         for c in range(4):
-            at = 4 * z + c
+            at = 4 * i + c
             xs_u[at:at + 1, :cols] = cons[z, c, 0:1, :]
             xs_d[at:at + 1, :cols] = cons[z, c, rows - 1:rows, :]
     for r in range(2):
@@ -108,9 +115,6 @@
             send[2 * r:2 * r + 1, cols:cols + 128] = direc[row:row + 1, :128]
             send[2 * r + 1:2 * r + 2, cols:cols + half - 128] = direc[row:row + 1, 128:]
 
-    waits = sum((has.astype(jnp.int32) for has, _ in greet), jnp.int32(1))
-    pl.semaphore_wait(barrier, waits)
-    to_z.start()
     for has, copy in ((has_d, to_xu), (has_u, to_xd), (has_r, to_yl), (has_l, to_yr)):
         @pl.when(has)
         def _():
@@ -150,55 +154,67 @@
         @pl.when(jnp.logical_not(has))
         def _():
             buffer[...] = jnp.zeros_like(buffer)
-    to_z.wait_recv()
-    for load in loads[6:]:
-        load.wait()
-
     row_at = lax.broadcasted_iota(jnp.int32, (rows, cols), 0)
-    own = [[cons[z, c] for c in range(4)] for z in range(2)]
-    layer = [zr[c] for c in range(4)]
-    below = [jnp.where(low, 0.0, a) for a in layer]
-    above = [jnp.where(low, a, 0.0) for a in layer]
-    stack = [below, own[0], own[1], above]
+    own = [[cons[z, c] for c in range(4)] for z in (near, far)]
     total = [[None] * 3 for _ in range(2)]
-    z_visc = [stack[i][3] + stack[i + 1][3] for i in range(3)]
+    visc_z = own[0][3] + own[1][3]
     for c in range(3):
-        flux = [z_visc[i] * (stack[i + 1][c] - stack[i][c]) for i in range(3)]
-        for z in range(2):
-            total[z][c] = flux[z] - flux[z + 1]
-    for z in range(2):
+        flux = visc_z * (own[0][c] - own[1][c])
+        total[0][c] = flux
+        total[1][c] = own[1][3] * own[1][c] - flux
+    for i, z in enumerate((near, far)):
         up_of, down_of, ext, ext_next = [], [], [], []
         for c in range(4):
-            at = 4 * z + c
-            a = own[z][c]
+            at = 4 * i + c
+            a = own[i][c]
             up_of.append(jnp.where(row_at == 0, xr_u[at:at + 1, :cols], shift(a, 1, 0)))
             down_of.append(jnp.where(row_at == rows - 1, xr_d[at:at + 1, :cols], shift(a, -1, 0)))
             wide_a = jnp.concatenate([yr_l[z, c], a, yr_r[z, c]], axis=1)
             ext.append(wide_a)
             ext_next.append(shift(wide_a, -1, 1))
-        visc_u, visc_d = own[z][3] + up_of[3], own[z][3] + down_of[3]
+        visc_u, visc_d = own[i][3] + up_of[3], own[i][3] + down_of[3]
         visc_y = ext[3] + ext_next[3]
         for c in range(3):
-            a = own[z][c]
+            a = own[i][c]
             flux = visc_y * (ext[c] - ext_next[c])
-            total[z][c] = 0.5 * (
-                total[z][c]
+            total[i][c] = (
+                total[i][c]
                 + visc_u * (a - up_of[c])
                 + visc_d * (a - down_of[c])
                 + (flux - shift(flux, 1, 1))[:, 128:128 + cols]
             )
+
+    for load in loads[6:]:
+        load.wait()
     sums = [None] * 3
-    for z in range(2):
-        for c in range(3):
-            for k in range(3):
-                image = (
-                    block[0][k] * total[z][c][:, tiles[0]]
-                    + block[1][k] * total[z][c][:, tiles[1]]
-                    + block[2][k] * total[z][c][:, tiles[2]]
-                )
-                out[c, z, :, tiles[k]] = image
-                term = image * adj[c, z, :, tiles[k]]
-                sums[k] = term if sums[k] is None else sums[k] + term
+
+    def finish(applied, c, z):
+        applied = 0.5 * applied
+        for k in range(3):
+            image = (
+                block[0][k] * applied[:, tiles[0]]
+                + block[1][k] * applied[:, tiles[1]]
+                + block[2][k] * applied[:, tiles[2]]
+            )
+            out[c, z, :, tiles[k]] = image
+            term = image * adj[c, z, :, tiles[k]]
+            sums[k] = term if sums[k] is None else sums[k] + term
+
+    for c in range(3):
+        finish(total[1][c], c, far)
+    to_zv.wait_recv()
+    visc_z = own[0][3] + zr[3]
+    to_z.wait_recv()
+    for c in range(3):
+        slots = [zr[c, :, tile] for tile in tiles]
+        layer = jnp.concatenate(
+            [
+                block[m][0] * slots[0] + block[m][1] * slots[1] + block[m][2] * slots[2]
+                for m in range(3)
+            ],
+            axis=1,
+        )
+        finish(total[0][c] + visc_z * (own[0][c] - layer), c, near)
     sums = jnp.concatenate(sums, axis=1)
     first, second = sums[:, :half], sums[:, half:]
     ps[...] = jnp.where(low, second, first)
@@ -235,7 +251,7 @@
     to_ps.wait_recv()
     hess[...] = REG * twice + scale * (mine + pr[...])
 
-    for copy in (to_z, to_cp, to_ps):
+    for copy in (to_z, to_zv, to_cp, to_ps):
         copy.wait_send()
     for has, copy in (
         (has_d, to_xu), (has_u, to_xd), (has_r, to_yl), (has_l, to_yr), (has_c, to_cc)
@@ -300,8 +316,8 @@
             vmem(direction.shape, f32),
             vmem(direction.shape, f32),
             pltpu.SemaphoreType.DMA((9,)),
-            pltpu.SemaphoreType.DMA((8,)),
-            pltpu.SemaphoreType.DMA((8,)),
+            pltpu.SemaphoreType.DMA((9,)),
+            pltpu.SemaphoreType.DMA((9,)),
         ],
         compiler_params=pltpu.CompilerParams(collective_id=0, has_side_effects=True, vmem_limit_bytes=LIMIT),
         cost_estimate=pl.CostEstimate(flops=200_000, bytes_accessed=400_000, transcendentals=1536),

time: 11.6 us -> 11.7 us (level)
  Pallas kernels: 10.7 us -> 10.9 us
    pallas_call x1, Pallas kernels: 10.1 us -> 10.2 us  [local(): pl.pallas_call(functools.partial(kernel, sizes), out_shape=(vmem(velocity...]
where the time goes in v3:
time: 11.7 us; the launch traced here: 11.5 us
  Pallas kernels  10.9 us (93%)
  between operations  0.64 us (5%)
    pallas_call x1, Pallas kernels, local(): pl.pallas_call(functools.partial(kernel, sizes), out_shape=(vmem(velocity...  10.2 us
    pallas_call x1, Pallas kernels, local(): pl.pallas_call(store, out_shape=(jax.ShapeDtypeStruct(velocity.shape, f32...  0.65 us

profile of v3, /device:TPU:0, one launch (start us, length us, event | category | flops | bytes accessed | tf_op | source)
XLA Modules:
  0.0 11.5 jit_solution(9454413040758589312)
XLA Ops:
  0.6 10.2 %hessian_apply.1 = (f32[3,2,8,384]{3,2,1,0:T(8,128)S(1)}, f32[8,192]{1,0:T(8,128)S(1)}) custom-call(f32[3,2,8,384]{3,2,1,0:T(8,128)} %vel_h.1, f32[3,2,8,384]{3,2,1,0:T(8,128)} %adj_h.1, f32[2,8,384]{2,1,0:T(8,128)} %visc_h.1, s32[8,128]{1,0:T(8,128)} %flags_h.1, s32[8,128]{1,0:T(8,128)} %index_h.1, f32[3,3,8]{2,1,0:T(4,128)} %bitcast.1, f32[8,192]{1,0:T(8,128)} %fric_h.1, ...), custom_call_target="tpu_custom_call" | custom-call | flops 200000 | bytes 400000 | tf_op jit(solution)/shard_map/hessian_apply/pallas_call | solution.py:289
  10.9 0.7 %store.1 = (f32[3,2,8,384]{3,2,1,0:T(8,128)}, f32[8,192]{1,0:T(8,128)}) custom-call(f32[3,2,8,384]{3,2,1,0:T(8,128)S(1)} %get-tuple-element.4.image_v, f32[8,192]{1,0:T(8,128)S(1)} %get-tuple-element.5.hess_v), custom_call_target="tpu_custom_call" | custom-call | tf_op jit(solution)/shard_map/store/pallas_call | solution.py:326

commit v4 on v3

--- a/solution.py
+++ b/solution.py
@@ -46,7 +46,7 @@
             )
         )
     ]
-    for load in loads:
+    for load in loads[:5]:
         load.start()
 
     up = {"gx": (gx + ngx - 1) % ngx}
@@ -63,6 +63,18 @@
         @pl.when(has)
         def _():
             pl.semaphore_signal(barrier, inc=1, device_id=device, device_id_type=MESH)
+
+    for load in loads[5:]:
+        load.start()
+
+    big[...] = jnp.zeros_like(big)
+    for has, buffers in (
+        (has_u, (xr_u,)), (has_d, (xr_d,)), (has_l, (yr_l,)), (has_r, (yr_r,)), (has_c, (cr_c,))
+    ):
+        @pl.when(jnp.logical_not(has))
+        def _():
+            for buffer in buffers:
+                buffer[...] = jnp.zeros_like(buffer)
 
     def remote(src, dst, at, device):
         return pltpu.make_async_remote_copy(
@@ -119,17 +131,31 @@
         @pl.when(has)
         def _():
             copy.start()
-
-    big[...] = jnp.zeros_like(big)
-    for has, copy, buffer in ((has_u, to_xu, xr_u), (has_d, to_xd, xr_d)):
+    big[rows:2 * rows, 128:128 + half] = direc[...]
+
+    row_at = lax.broadcasted_iota(jnp.int32, (rows, cols), 0)
+    lane_at = lax.broadcasted_iota(jnp.int32, (rows, cols), 1)
+    inner_row, inner_lane = row_at < rows - 1, lane_at < cols - 1
+    own = [[cons[z, c] for c in range(4)] for z in (near, far)]
+    total = [[None] * 3 for _ in range(2)]
+    visc_z = own[0][3] + own[1][3]
+    for c in range(3):
+        flux = visc_z * (own[0][c] - own[1][c])
+        total[0][c] = flux
+        total[1][c] = own[1][3] * own[1][c] - flux
+    for i in range(2):
+        for axis, inner in ((0, inner_row), (1, inner_lane)):
+            visc = own[i][3]
+            visc = jnp.where(inner, visc + shift(visc, -1, axis), 0.0)
+            for c in range(3):
+                a = own[i][c]
+                flux = visc * (a - shift(a, -1, axis))
+                total[i][c] = total[i][c] + flux - shift(flux, 1, axis)
+
+    for has, copy in ((has_u, to_xu), (has_d, to_xd)):
         @pl.when(has)
         def _():
             copy.wait_recv()
-
-        @pl.when(jnp.logical_not(has))
-        def _():
-            buffer[...] = jnp.zeros_like(buffer)
-    big[rows:2 * rows, 128:128 + half] = direc[...]
     for buffer, row in ((xr_u, rows - 2), (xr_d, 2 * rows)):
         for r in range(2):
             big[row + r:row + r + 1, 128:256] = buffer[2 * r:2 * r + 1, cols:cols + 128]
@@ -146,56 +172,35 @@
     def _():
         to_cc.start()
 
-    for has, copy, buffer in ((has_l, to_yl, yr_l), (has_r, to_yr, yr_r)):
+    for sent, got, row in ((xs_u, xr_u, 0), (xs_d, xr_d, rows - 1)):
+        mine, other = sent[:, :cols], got[:, :cols]
+        gap, visc = mine - other, mine + other
+        for i in range(2):
+            for c in range(3):
+                flux = visc[4 * i + 3:4 * i + 4] * gap[4 * i + c:4 * i + c + 1]
+                total[i][c] = total[i][c] + jnp.where(row_at == row, flux, 0.0)
+    for has, copy in ((has_l, to_yl), (has_r, to_yr)):
         @pl.when(has)
         def _():
             copy.wait_recv()
-
-        @pl.when(jnp.logical_not(has))
-        def _():
-            buffer[...] = jnp.zeros_like(buffer)
-    row_at = lax.broadcasted_iota(jnp.int32, (rows, cols), 0)
-    own = [[cons[z, c] for c in range(4)] for z in (near, far)]
-    total = [[None] * 3 for _ in range(2)]
-    visc_z = own[0][3] + own[1][3]
-    for c in range(3):
-        flux = visc_z * (own[0][c] - own[1][c])
-        total[0][c] = flux
-        total[1][c] = own[1][3] * own[1][c] - flux
-    for i, z in enumerate((near, far)):
-        up_of, down_of, ext, ext_next = [], [], [], []
-        for c in range(4):
-            at = 4 * i + c
-            a = own[i][c]
-            up_of.append(jnp.where(row_at == 0, xr_u[at:at + 1, :cols], shift(a, 1, 0)))
-            down_of.append(jnp.where(row_at == rows - 1, xr_d[at:at + 1, :cols], shift(a, -1, 0)))
-            wide_a = jnp.concatenate([yr_l[z, c], a, yr_r[z, c]], axis=1)
-            ext.append(wide_a)
-            ext_next.append(shift(wide_a, -1, 1))
-        visc_u, visc_d = own[i][3] + up_of[3], own[i][3] + down_of[3]
-        visc_y = ext[3] + ext_next[3]
-        for c in range(3):
-            a = own[i][c]
-            flux = visc_y * (ext[c] - ext_next[c])
-            total[i][c] = (
-                total[i][c]
-                + visc_u * (a - up_of[c])
-                + visc_d * (a - down_of[c])
-                + (flux - shift(flux, 1, 1))[:, 128:128 + cols]
-            )
+    total = [[[total[i][c][:, tile] for tile in tiles] for c in range(3)] for i in range(2)]
+    lane = lax.broadcasted_iota(jnp.int32, (rows, 128), 1)
+    for got, by, at, m in ((yr_l, 1, 0, 0), (yr_r, -1, 127, 2)):
+        for i, z in enumerate((near, far)):
+            visc = own[i][3][:, tiles[m]] + shift(got[z, 3], by, 1)
+            visc = jnp.where(lane == at, visc, 0.0)
+            for c in range(3):
+                gap = own[i][c][:, tiles[m]] - shift(got[z, c], by, 1)
+                total[i][c][m] = total[i][c][m] + visc * gap
 
     for load in loads[6:]:
         load.wait()
     sums = [None] * 3
 
     def finish(applied, c, z):
-        applied = 0.5 * applied
+        applied = [0.5 * a for a in applied]
         for k in range(3):
-            image = (
-                block[0][k] * applied[:, tiles[0]]
-                + block[1][k] * applied[:, tiles[1]]
-                + block[2][k] * applied[:, tiles[2]]
-            )
+            image = block[0][k] * applied[0] + block[1][k] * applied[1] + block[2][k] * applied[2]
             out[c, z, :, tiles[k]] = image
             term = image * adj[c, z, :, tiles[k]]
             sums[k] = term if sums[k] is None else sums[k] + term
@@ -207,14 +212,18 @@
     to_z.wait_recv()
     for c in range(3):
         slots = [zr[c, :, tile] for tile in tiles]
-        layer = jnp.concatenate(
+        layer = [
+            block[m][0] * slots[0] + block[m][1] * slots[1] + block[m][2] * slots[2]
+            for m in range(3)
+        ]
+        finish(
             [
-                block[m][0] * slots[0] + block[m][1] * slots[1] + block[m][2] * slots[2]
+                total[0][c][m] + visc_z[:, tiles[m]] * (own[0][c][:, tiles[m]] - layer[m])
                 for m in range(3)
             ],
-            axis=1,
+            c,
+            near,
         )
-        finish(total[0][c] + visc_z * (own[0][c] - layer), c, near)
     sums = jnp.concatenate(sums, axis=1)
     first, second = sums[:, :half], sums[:, half:]
     ps[...] = jnp.where(low, second, first)
@@ -226,10 +235,6 @@
     @pl.when(has_c)
     def _():
         to_cc.wait_recv()
-
-    @pl.when(jnp.logical_not(has_c))
-    def _():
-        cr_c[...] = jnp.zeros_like(cr_c)
 
     from_p, from_c = cr_p[...], cr_c[...]
     from_low = jnp.where(low, from_c, from_p)

time: 11.7 us -> 11.6 us (level)
  no operation moved by 1% of the time
where the time goes in v4:
time: 11.6 us; the launch traced here: 11.4 us
  Pallas kernels  10.8 us (93%)
  between operations  0.64 us (6%)
    pallas_call x1, Pallas kernels, local(): pl.pallas_call(functools.partial(kernel, sizes), out_shape=(vmem(velocity...  10.1 us
    pallas_call x1, Pallas kernels, local(): pl.pallas_call(store, out_shape=(jax.ShapeDtypeStruct(velocity.shape, f32...  0.65 us

profile of v4, /device:TPU:0, one launch (start us, length us, event | category | flops | bytes accessed | tf_op | source)
XLA Modules:
  0.0 11.4 jit_solution(363968570536256002)
XLA Ops:
  0.6 10.1 %hessian_apply.1 = (f32[3,2,8,384]{3,2,1,0:T(8,128)S(1)}, f32[8,192]{1,0:T(8,128)S(1)}) custom-call(f32[3,2,8,384]{3,2,1,0:T(8,128)} %vel_h.1, f32[3,2,8,384]{3,2,1,0:T(8,128)} %adj_h.1, f32[2,8,384]{2,1,0:T(8,128)} %visc_h.1, s32[8,128]{1,0:T(8,128)} %flags_h.1, s32[8,128]{1,0:T(8,128)} %index_h.1, f32[3,3,8]{2,1,0:T(4,128)} %bitcast.1, f32[8,192]{1,0:T(8,128)} %fric_h.1, ...), custom_call_target="tpu_custom_call" | custom-call | flops 200000 | bytes 400000 | tf_op jit(solution)/shard_map/hessian_apply/pallas_call | solution.py:294
  10.8 0.7 %store.1 = (f32[3,2,8,384]{3,2,1,0:T(8,128)}, f32[8,192]{1,0:T(8,128)}) custom-call(f32[3,2,8,384]{3,2,1,0:T(8,128)S(1)} %get-tuple-element.4.image_v, f32[8,192]{1,0:T(8,128)S(1)} %get-tuple-element.5.hess_v), custom_call_target="tpu_custom_call" | custom-call | tf_op jit(solution)/shard_map/store/pallas_call | solution.py:331

commit v5 on v4

--- a/solution.py
+++ b/solution.py
@@ -11,7 +11,7 @@
 REG = 0.05
 LIMIT = 4 * 1024 * 1024
 MESH = pl.DeviceIdType.MESH
-XU, XD, YL, YR, ZZ, ZV, CP, CC, PS = range(9)
+XU, XD, YL, YR, ZZ, CP, CC, PS = range(8)
 
 
 def shift(value, by, axis):
@@ -46,8 +46,6 @@
             )
         )
     ]
-    for load in loads[:5]:
-        load.start()
 
     up = {"gx": (gx + ngx - 1) % ngx}
     down = {"gx": (gx + 1) % ngx}
@@ -64,7 +62,7 @@
         def _():
             pl.semaphore_signal(barrier, inc=1, device_id=device, device_id_type=MESH)
 
-    for load in loads[5:]:
+    for load in loads:
         load.start()
 
     big[...] = jnp.zeros_like(big)
@@ -87,16 +85,10 @@
     to_yl = remote(cons.at[:, :, :, cols - 128:], yr_l, YL, right)
     to_yr = remote(cons.at[:, :, :, :128], yr_r, YR, left)
     near, far = 1 - gz, gz
-    to_z = remote(vel_h.at[:, near], zr.at[:3], ZZ, partner)
-    to_zv = remote(visc_h.at[near], zr.at[3], ZV, partner)
+    to_z = remote(cons.at[near], zr, ZZ, partner)
     to_cp = remote(cs_p, cr_p, CP, partner)
     to_cc = remote(cs_c, cr_c, CC, cross)
     to_ps = remote(ps, pr, PS, partner)
-
-    waits = sum((has.astype(jnp.int32) for has, _ in greet), jnp.int32(1))
-    pl.semaphore_wait(barrier, waits)
-    to_z.start()
-    to_zv.start()
 
     for load in loads[:6]:
         load.wait()
@@ -127,11 +119,14 @@
             send[2 * r:2 * r + 1, cols:cols + 128] = direc[row:row + 1, :128]
             send[2 * r + 1:2 * r + 2, cols:cols + half - 128] = direc[row:row + 1, 128:]
 
+    big[rows:2 * rows, 128:128 + half] = direc[...]
+    waits = sum((has.astype(jnp.int32) for has, _ in greet), jnp.int32(1))
+    pl.semaphore_wait(barrier, waits)
+    to_z.start()
     for has, copy in ((has_d, to_xu), (has_u, to_xd), (has_r, to_yl), (has_l, to_yr)):
         @pl.when(has)
         def _():
             copy.start()
-    big[rows:2 * rows, 128:128 + half] = direc[...]
 
     row_at = lax.broadcasted_iota(jnp.int32, (rows, cols), 0)
     lane_at = lax.broadcasted_iota(jnp.int32, (rows, cols), 1)
@@ -207,23 +202,11 @@
 
     for c in range(3):
         finish(total[1][c], c, far)
-    to_zv.wait_recv()
+    to_z.wait_recv()
     visc_z = own[0][3] + zr[3]
-    to_z.wait_recv()
     for c in range(3):
-        slots = [zr[c, :, tile] for tile in tiles]
-        layer = [
-            block[m][0] * slots[0] + block[m][1] * slots[1] + block[m][2] * slots[2]
-            for m in range(3)
-        ]
-        finish(
-            [
-                total[0][c][m] + visc_z[:, tiles[m]] * (own[0][c][:, tiles[m]] - layer[m])
-                for m in range(3)
-            ],
-            c,
-            near,
-        )
+        flux = visc_z * (own[0][c] - zr[c])
+        finish([total[0][c][m] + flux[:, tiles[m]] for m in range(3)], c, near)
     sums = jnp.concatenate(sums, axis=1)
     first, second = sums[:, :half], sums[:, half:]
     ps[...] = jnp.where(low, second, first)
@@ -256,7 +239,7 @@
     to_ps.wait_recv()
     hess[...] = REG * twice + scale * (mine + pr[...])
 
-    for copy in (to_z, to_zv, to_cp, to_ps):
+    for copy in (to_z, to_cp, to_ps):
         copy.wait_send()
     for has, copy in (
         (has_d, to_xu), (has_u, to_xd), (has_r, to_yl), (has_l, to_yr), (has_c, to_cc)
@@ -321,8 +304,8 @@
             vmem(direction.shape, f32),
             vmem(direction.shape, f32),
             pltpu.SemaphoreType.DMA((9,)),
-            pltpu.SemaphoreType.DMA((9,)),
-            pltpu.SemaphoreType.DMA((9,)),
+            pltpu.SemaphoreType.DMA((8,)),
+            pltpu.SemaphoreType.DMA((8,)),
         ],
         compiler_params=pltpu.CompilerParams(collective_id=0, has_side_effects=True, vmem_limit_bytes=LIMIT),
         cost_estimate=pl.CostEstimate(flops=200_000, bytes_accessed=400_000, transcendentals=1536),

time: 11.6 us -> 11.5 us (level)
  no operation moved by 1% of the time
where the time goes in v5:
time: 11.5 us; the launch traced here: 11.3 us
  Pallas kernels  10.7 us (93%)
  between operations  0.64 us (6%)
    pallas_call x1, Pallas kernels, local(): pl.pallas_call(functools.partial(kernel, sizes), out_shape=(vmem(velocity...  10 us
    pallas_call x1, Pallas kernels, local(): pl.pallas_call(store, out_shape=(jax.ShapeDtypeStruct(velocity.shape, f32...  0.65 us

profile of v5, /device:TPU:0, one launch (start us, length us, event | category | flops | bytes accessed | tf_op | source)
XLA Modules:
  0.0 11.3 jit_solution(1146259174956979393)
XLA Ops:
  0.6 10.0 %hessian_apply.1 = (f32[3,2,8,384]{3,2,1,0:T(8,128)S(1)}, f32[8,192]{1,0:T(8,128)S(1)}) custom-call(f32[3,2,8,384]{3,2,1,0:T(8,128)} %vel_h.1, f32[3,2,8,384]{3,2,1,0:T(8,128)} %adj_h.1, f32[2,8,384]{2,1,0:T(8,128)} %visc_h.1, s32[8,128]{1,0:T(8,128)} %flags_h.1, s32[8,128]{1,0:T(8,128)} %index_h.1, f32[3,3,8]{2,1,0:T(4,128)} %bitcast.1, f32[8,192]{1,0:T(8,128)} %fric_h.1, ...), custom_call_target="tpu_custom_call" | custom-call | flops 200000 | bytes 400000 | tf_op jit(solution)/shard_map/hessian_apply/pallas_call | solution.py:277
  10.7 0.7 %store.1 = (f32[3,2,8,384]{3,2,1,0:T(8,128)}, f32[8,192]{1,0:T(8,128)}) custom-call(f32[3,2,8,384]{3,2,1,0:T(8,128)S(1)} %get-tuple-element.4.image_v, f32[8,192]{1,0:T(8,128)S(1)} %get-tuple-element.5.hess_v), custom_call_target="tpu_custom_call" | custom-call | tf_op jit(solution)/shard_map/store/pallas_call | solution.py:314

commit v6 on v5

--- a/solution.py
+++ b/solution.py
@@ -213,6 +213,16 @@
     to_ps.start()
     mine = jnp.where(low, first, second)
 
+    scale = mask[...].astype(jnp.float32) * jnp.exp(fric[...])
+    row_g = gx * rows - rows + lax.broadcasted_iota(jnp.int32, wide.shape, 0)
+    col_g = (gy * ngz + gz) * half - 128 + lax.broadcasted_iota(jnp.int32, wide.shape, 1)
+    inside = (row_g >= 0) & (row_g < ngx * rows) & (col_g >= 0) & (col_g < ngy * ngz * half)
+    base = scale * mine
+    to_z.wait_send()
+    for has, copy in ((has_d, to_xu), (has_u, to_xd), (has_r, to_yl), (has_l, to_yr)):
+        @pl.when(has)
+        def _():
+            copy.wait_send()
     to_cp.wait_recv()
 
     @pl.when(has_c)
@@ -230,23 +240,18 @@
     def laplace(v):
         return 4.0 * v - shift(v, 1, 0) - shift(v, -1, 0) - shift(v, 1, 1) - shift(v, -1, 1)
 
-    row_g = gx * rows - rows + lax.broadcasted_iota(jnp.int32, wide.shape, 0)
-    col_g = (gy * ngz + gz) * half - 128 + lax.broadcasted_iota(jnp.int32, wide.shape, 1)
-    inside = (row_g >= 0) & (row_g < ngx * rows) & (col_g >= 0) & (col_g < ngy * ngz * half)
     twice = laplace(jnp.where(inside, laplace(wide), 0.0))[rows:2 * rows, 128:128 + half]
-    scale = mask[...].astype(jnp.float32) * jnp.exp(fric[...])
-
+
+    base = REG * twice + base
+    to_cp.wait_send()
+
+    @pl.when(has_c)
+    def _():
+        to_cc.wait_send()
+
+    to_ps.wait_send()
     to_ps.wait_recv()
-    hess[...] = REG * twice + scale * (mine + pr[...])
-
-    for copy in (to_z, to_cp, to_ps):
-        copy.wait_send()
-    for has, copy in (
-        (has_d, to_xu), (has_u, to_xd), (has_r, to_yl), (has_l, to_yr), (has_c, to_cc)
-    ):
-        @pl.when(has)
-        def _():
-            copy.wait_send()
+    hess[...] = base + scale * pr[...]
 
 
 def store(image_v, hess_v, image_h, hess_h, sem):

time: 11.5 us -> 11.5 us (level)
  no operation moved by 1% of the time
where the time goes in v6:
time: 11.5 us; the launch traced here: 11.3 us
  Pallas kernels  10.7 us (93%)
  between operations  0.64 us (6%)
    pallas_call x1, Pallas kernels, local(): pl.pallas_call(functools.partial(kernel, sizes), out_shape=(vmem(velocity...  10 us
    pallas_call x1, Pallas kernels, local(): pl.pallas_call(store, out_shape=(jax.ShapeDtypeStruct(velocity.shape, f32...  0.65 us

profile of v6, /device:TPU:0, one launch (start us, length us, event | category | flops | bytes accessed | tf_op | source)
XLA Modules:
  0.0 11.3 jit_solution(2677164082713440136)
XLA Ops:
  0.6 10.0 %hessian_apply.1 = (f32[3,2,8,384]{3,2,1,0:T(8,128)S(1)}, f32[8,192]{1,0:T(8,128)S(1)}) custom-call(f32[3,2,8,384]{3,2,1,0:T(8,128)} %vel_h.1, f32[3,2,8,384]{3,2,1,0:T(8,128)} %adj_h.1, f32[2,8,384]{2,1,0:T(8,128)} %visc_h.1, s32[8,128]{1,0:T(8,128)} %flags_h.1, s32[8,128]{1,0:T(8,128)} %index_h.1, f32[3,3,8]{2,1,0:T(4,128)} %bitcast.1, f32[8,192]{1,0:T(8,128)} %fric_h.1, ...), custom_call_target="tpu_custom_call" | custom-call | flops 200000 | bytes 400000 | tf_op jit(solution)/shard_map/hessian_apply/pallas_call | solution.py:282
  10.7 0.7 %store.1 = (f32[3,2,8,384]{3,2,1,0:T(8,128)}, f32[8,192]{1,0:T(8,128)}) custom-call(f32[3,2,8,384]{3,2,1,0:T(8,128)S(1)} %get-tuple-element.4.image_v, f32[8,192]{1,0:T(8,128)S(1)} %get-tuple-element.5.hess_v), custom_call_target="tpu_custom_call" | custom-call | tf_op jit(solution)/shard_map/store/pallas_call | solution.py:319

commit v7 on v6

--- a/solution.py
+++ b/solution.py
@@ -11,7 +11,7 @@
 REG = 0.05
 LIMIT = 4 * 1024 * 1024
 MESH = pl.DeviceIdType.MESH
-XU, XD, YL, YR, ZZ, CP, CC, PS = range(8)
+XU, XD, YL, YR, CP, CC, PS, ZZ = range(8)
 
 
 def shift(value, by, axis):
@@ -85,7 +85,7 @@
     to_yl = remote(cons.at[:, :, :, cols - 128:], yr_l, YL, right)
     to_yr = remote(cons.at[:, :, :, :128], yr_r, YR, left)
     near, far = 1 - gz, gz
-    to_z = remote(cons.at[near], zr, ZZ, partner)
+    to_z = [remote(cons.at[near, c], zr.at[c], ZZ + c, partner) for c in range(4)]
     to_cp = remote(cs_p, cr_p, CP, partner)
     to_cc = remote(cs_c, cr_c, CC, cross)
     to_ps = remote(ps, pr, PS, partner)
@@ -122,7 +122,8 @@
     big[rows:2 * rows, 128:128 + half] = direc[...]
     waits = sum((has.astype(jnp.int32) for has, _ in greet), jnp.int32(1))
     pl.semaphore_wait(barrier, waits)
-    to_z.start()
+    for c in (3, 0, 1, 2):
+        to_z[c].start()
     for has, copy in ((has_d, to_xu), (has_u, to_xd), (has_r, to_yl), (has_l, to_yr)):
         @pl.when(has)
         def _():
@@ -202,9 +203,10 @@
 
     for c in range(3):
         finish(total[1][c], c, far)
-    to_z.wait_recv()
+    to_z[3].wait_recv()
     visc_z = own[0][3] + zr[3]
     for c in range(3):
+        to_z[c].wait_recv()
         flux = visc_z * (own[0][c] - zr[c])
         finish([total[0][c][m] + flux[:, tiles[m]] for m in range(3)], c, near)
     sums = jnp.concatenate(sums, axis=1)
@@ -218,7 +220,8 @@
     col_g = (gy * ngz + gz) * half - 128 + lax.broadcasted_iota(jnp.int32, wide.shape, 1)
     inside = (row_g >= 0) & (row_g < ngx * rows) & (col_g >= 0) & (col_g < ngy * ngz * half)
     base = scale * mine
-    to_z.wait_send()
+    for copy in to_z:
+        copy.wait_send()
     for has, copy in ((has_d, to_xu), (has_u, to_xd), (has_r, to_yl), (has_l, to_yr)):
         @pl.when(has)
         def _():
@@ -256,9 +259,11 @@
 
 def store(image_v, hess_v, image_h, hess_h, sem):
     copies = [
-        pltpu.make_async_copy(image_v, image_h, sem.at[0]),
-        pltpu.make_async_copy(hess_v, hess_h, sem.at[1]),
+        pltpu.make_async_copy(image_v.at[c, z], image_h.at[c, z], sem.at[2 * c + z])
+        for c in range(3)
+        for z in range(2)
     ]
+    copies.append(pltpu.make_async_copy(hess_v, hess_h, sem.at[6]))
     for copy in copies:
         copy.start()
     for copy in copies:
@@ -309,8 +314,8 @@
             vmem(direction.shape, f32),
             vmem(direction.shape, f32),
             pltpu.SemaphoreType.DMA((9,)),
-            pltpu.SemaphoreType.DMA((8,)),
-            pltpu.SemaphoreType.DMA((8,)),
+            pltpu.SemaphoreType.DMA((11,)),
+            pltpu.SemaphoreType.DMA((11,)),
         ],
         compiler_params=pltpu.CompilerParams(collective_id=0, has_side_effects=True, vmem_limit_bytes=LIMIT),
         cost_estimate=pl.CostEstimate(flops=200_000, bytes_accessed=400_000, transcendentals=1536),
@@ -324,7 +329,7 @@
         ),
         in_specs=[pl.BlockSpec(memory_space=vmem)] * 2,
         out_specs=(anywhere,) * 2,
-        scratch_shapes=[pltpu.SemaphoreType.DMA((2,))],
+        scratch_shapes=[pltpu.SemaphoreType.DMA((7,))],
         compiler_params=pltpu.CompilerParams(vmem_limit_bytes=LIMIT),
         name="store",
     )(image, hess)

time: 11.5 us -> 11.6 us (level)
  no operation moved by 1% of the time
where the time goes in v7:
time: 11.6 us; the launch traced here: 11.4 us
  Pallas kernels  10.8 us (93%)
  between operations  0.64 us (6%)
    pallas_call x1, Pallas kernels, local(): pl.pallas_call(functools.partial(kernel, sizes), out_shape=(vmem(velocity...  10.1 us
    pallas_call x1, Pallas kernels, local(): pl.pallas_call(store, out_shape=(jax.ShapeDtypeStruct(velocity.shape, f32...  0.69 us

profile of v7, /device:TPU:0, one launch (start us, length us, event | category | flops | bytes accessed | tf_op | source)
XLA Modules:
  0.0 11.4 jit_solution(7365425614288586128)
XLA Ops:
  0.6 10.1 %hessian_apply.1 = (f32[3,2,8,384]{3,2,1,0:T(8,128)S(1)}, f32[8,192]{1,0:T(8,128)S(1)}) custom-call(f32[3,2,8,384]{3,2,1,0:T(8,128)} %vel_h.1, f32[3,2,8,384]{3,2,1,0:T(8,128)} %adj_h.1, f32[2,8,384]{2,1,0:T(8,128)} %visc_h.1, s32[8,128]{1,0:T(8,128)} %flags_h.1, s32[8,128]{1,0:T(8,128)} %index_h.1, f32[3,3,8]{2,1,0:T(4,128)} %bitcast.1, f32[8,192]{1,0:T(8,128)} %fric_h.1, ...), custom_call_target="tpu_custom_call" | custom-call | flops 200000 | bytes 400000 | tf_op jit(solution)/shard_map/hessian_apply/pallas_call | solution.py:287
  10.7 0.7 %store.1 = (f32[3,2,8,384]{3,2,1,0:T(8,128)}, f32[8,192]{1,0:T(8,128)}) custom-call(f32[3,2,8,384]{3,2,1,0:T(8,128)S(1)} %get-tuple-element.4.image_v, f32[8,192]{1,0:T(8,128)S(1)} %get-tuple-element.5.hess_v), custom_call_target="tpu_custom_call" | custom-call | tf_op jit(solution)/shard_map/store/pallas_call | solution.py:324

commit v8 on v6

--- a/solution.py
+++ b/solution.py
@@ -122,8 +122,12 @@
     big[rows:2 * rows, 128:128 + half] = direc[...]
     waits = sum((has.astype(jnp.int32) for has, _ in greet), jnp.int32(1))
     pl.semaphore_wait(barrier, waits)
+    for has, copy in ((has_d, to_xu), (has_u, to_xd)):
+        @pl.when(has)
+        def _():
+            copy.start()
     to_z.start()
-    for has, copy in ((has_d, to_xu), (has_u, to_xd), (has_r, to_yl), (has_l, to_yr)):
+    for has, copy in ((has_r, to_yl), (has_l, to_yr)):
         @pl.when(has)
         def _():
             copy.start()

time: 11.5 us -> 11.5 us (level)
  no operation moved by 1% of the time
where the time goes in v8:
time: 11.5 us; the launch traced here: 11.3 us
  Pallas kernels  10.7 us (93%)
  between operations  0.64 us (6%)
    pallas_call x1, Pallas kernels, local(): pl.pallas_call(functools.partial(kernel, sizes), out_shape=(vmem(velocity...  10 us
    pallas_call x1, Pallas kernels, local(): pl.pallas_call(store, out_shape=(jax.ShapeDtypeStruct(velocity.shape, f32...  0.65 us

profile of v8, /device:TPU:0, one launch (start us, length us, event | category | flops | bytes accessed | tf_op | source)
XLA Modules:
  0.0 11.3 jit_solution(15751222327722276702)
XLA Ops:
  0.6 10.0 %hessian_apply.1 = (f32[3,2,8,384]{3,2,1,0:T(8,128)S(1)}, f32[8,192]{1,0:T(8,128)S(1)}) custom-call(f32[3,2,8,384]{3,2,1,0:T(8,128)} %vel_h.1, f32[3,2,8,384]{3,2,1,0:T(8,128)} %adj_h.1, f32[2,8,384]{2,1,0:T(8,128)} %visc_h.1, s32[8,128]{1,0:T(8,128)} %flags_h.1, s32[8,128]{1,0:T(8,128)} %index_h.1, f32[3,3,8]{2,1,0:T(4,128)} %bitcast.1, f32[8,192]{1,0:T(8,128)} %fric_h.1, ...), custom_call_target="tpu_custom_call" | custom-call | flops 200000 | bytes 400000 | tf_op jit(solution)/shard_map/hessian_apply/pallas_call | solution.py:286
  10.7 0.7 %store.1 = (f32[3,2,8,384]{3,2,1,0:T(8,128)}, f32[8,192]{1,0:T(8,128)}) custom-call(f32[3,2,8,384]{3,2,1,0:T(8,128)S(1)} %get-tuple-element.4.image_v, f32[8,192]{1,0:T(8,128)S(1)} %get-tuple-element.5.hess_v), custom_call_target="tpu_custom_call" | custom-call | tf_op jit(solution)/shard_map/store/pallas_call | solution.py:323
